TPU v7x, 128 devices: a whole 4x4x4 slice. The times are simulated.
128 devices in a mesh: ctx: 32 (over x, z, core), head: 4 (over y).
Axes of the slice: x: 4, y: 4, z: 4, core: 2. Of those that a mesh axis runs over, the one named last changes fastest.
Arguments:
- queries: bfloat16 [16384, 2048], P(('ctx', 'head')), may hold values from -240 to 240
- keys_in: bfloat16 [16384, 2048], P(('ctx', 'head')), may hold values from -8 to 8
- values: bfloat16 [16384, 2048], P(('ctx', 'head')), may hold values from -6 to 6
- out_grad: bfloat16 [16384, 2048], P(('ctx', 'head')), may hold values from -6 to 6
- doc_lengths: int32 [15], replicated, may hold values from 1 to 2048, 16384 in all
Outputs:
- attended: bfloat16 [16384, 2048], P(('ctx', 'head'))
- query_grad: bfloat16 [16384, 2048], P(('ctx', 'head'))
- key_grad: bfloat16 [16384, 2048], P(('ctx', 'head'))
- value_grad: bfloat16 [16384, 2048], P(('ctx', 'head'))
Inputs may be any that keep to these rules, and one draw needn't show every extreme that they name: `doc_lengths`: each document has 1 to 2048 tokens, the longest exactly 2048; the lengths sum to 16384.
All inputs are finite; a program needn't handle non-finite values.
Results may differ from a plain program's by a relative error of at most 0.035.
Values may be sent and summed in bfloat16 or wider, within the bound.
A program may use at most 192 MiB of HBM per device.

v0:
```python
import jax
import jax.numpy as jnp
from jax import lax
from jax.experimental import pallas as pl
from jax.experimental.pallas import tpu as pltpu
from jax.sharding import PartitionSpec as P

HEAD_DIM = 128
NDOCS = 15
GROUP = 2048
PIECE = 128
PIECES = GROUP // PIECE
B = 256
TILES = GROUP // B
FOLD = TILES + 1
NEG = -1e30
SCALE = HEAD_DIM ** (-0.5)
LOG2E = 1.4426950408889634
MESH = pl.DeviceIdType.MESH
BF = jnp.bfloat16
F32 = jnp.float32


def ctx_of(x, z, core):
    return (x * 4 + z) * 2 + core


def dot_nt(a, b):
    return lax.dot_general(a, b, (((1,), (1,)), ((), ())), preferred_element_type=F32)


def dot_nn(a, b):
    return lax.dot_general(a, b, (((1,), (0,)), ((), ())), preferred_element_type=F32)


def kernel(
    lens, q_in, k_in, v_in, g_in, att_out, dq_out, dk_out, dv_out,
    q_own, g_own, k_win, v_win, scores, probs, end_row, start_row, end_lane, peaks, invs,
    att, dq, grads, far_buf, sib_buf, far_in, sib_in, total,
    send, recv, hsend, hrecv, osend, orecv, fsend, frecv, ssend, srecv,
):
    ctx = lax.axis_index("ctx")
    y = lax.axis_index("head")
    x = ctx // 8
    z = (ctx // 2) % 4
    core = ctx % 2
    half = z // 2
    my_slot = ((2 * z + core) % 4) * 4 + y
    my_head = z * 4 + y
    sibling = {"ctx": ctx_of(x, z, 1 - core), "head": y}
    far_x = jnp.where(core == 0, (x + 3) % 4, (x + 1) % 4)
    beside = {"ctx": ctx_of(far_x, z, 1 - core), "head": y}
    barrier = pltpu.get_barrier_semaphore()

    def host_of(step):
        zz = (z + step // 4) % 4
        yy = (y + step % 4) % 4
        return zz * 4 + yy, {"ctx": ctx_of(x, zz, half), "head": yy}

    def owner_of(s):
        zz, cc, yy = 2 * core + s // 8, (s // 4) % 2, s % 4
        mine = (zz == z) & (cc == core) & (yy == y)
        return mine, {"ctx": ctx_of(x, zz, cc), "head": yy}

    def greet(step, c):
        _, host = host_of(step)

        @pl.when((step > 0) | (half != core))
        def _():
            pl.semaphore_signal(barrier, inc=1, device_id=host, device_id_type=MESH)

        mine, owner = owner_of(step)

        @pl.when(jnp.logical_not(mine))
        def _():
            pl.semaphore_signal(barrier, inc=1, device_id=owner, device_id_type=MESH)

        return c

    lax.fori_loop(0, PIECES, greet, 0)
    pl.semaphore_signal(barrier, inc=1, device_id=sibling, device_id_type=MESH)
    pl.semaphore_signal(barrier, inc=1, device_id=beside, device_id_type=MESH)
    pl.semaphore_wait(barrier, 2 * jnp.where(half == core, PIECES - 1, PIECES) + 2)

    def rows_of(s, count):
        return pl.ds(pl.multiple_of(s * count, count), count)

    own = pl.ds(GROUP, GROUP)
    incoming = (k_win.at[own], q_own, v_win.at[own], g_own)
    sources = (k_in, q_in, v_in, g_in)

    def in_refs(a, step):
        head, host = host_of(step)
        return sources[a].at[:, rows_of(head, HEAD_DIM)], incoming[a].at[rows_of(my_slot, PIECE)], host

    def in_copy(a, step):
        src, dst, host = in_refs(a, step)
        return pltpu.make_async_remote_copy(
            src_ref=src, dst_ref=dst, send_sem=send.at[a, step], recv_sem=recv.at[a, my_slot],
            device_id=host, device_id_type=MESH,
        )

    for a in range(4):

        @pl.when(half == core)
        def _():
            src, dst, _ = in_refs(a, 0)
            pltpu.make_async_copy(src, dst, recv.at[a, my_slot]).start()

        @pl.when(half != core)
        def _():
            in_copy(a, 0).start()

        def start_in(step, c):
            in_copy(a, step).start()
            return c

        lax.fori_loop(1, PIECES, start_in, 0)

    bound = -((ctx // 8) * 2 + core) * GROUP
    bounds = [bound]
    for j in range(NDOCS):
        bounds.append(bounds[-1] + lens[j])

    def find_bounds(i, c):
        pos = lax.broadcasted_iota(jnp.int32, (B, 128), 0) + i * B
        first = jnp.full((B, 128), bounds[0], jnp.int32)
        last = jnp.full((B, 128), bounds[NDOCS], jnp.int32)
        lane_pos = lax.broadcasted_iota(jnp.int32, (8, B), 1) + i * B
        lane_last = jnp.full((8, B), bounds[NDOCS], jnp.int32)
        for j in range(1, NDOCS):
            first = jnp.where(pos >= bounds[j], bounds[j], first)
            k = NDOCS - j
            last = jnp.where(pos < bounds[k], bounds[k], last)
            lane_last = jnp.where(lane_pos < bounds[k], bounds[k], lane_last)
        start_row[i] = first - i * B
        end_row[i] = last - i * B
        end_lane[i] = lane_last - i * B
        return c

    lax.fori_loop(0, TILES, find_bounds, 0)

    def clear(b, c):
        grads[0, b] = jnp.zeros((HEAD_DIM, B), F32)
        grads[1, b] = jnp.zeros((HEAD_DIM, B), F32)
        return c

    lax.fori_loop(0, 3 * TILES, clear, 0)

    def wait_in(a):
        def wait(s, c):
            piece = incoming[a].at[rows_of(s, PIECE)]
            pltpu.make_async_copy(piece, piece, recv.at[a, s]).wait()
            return c

        lax.fori_loop(0, PIECES, wait, 0)

    def halo_copies(a, win):
        sib = pltpu.make_async_remote_copy(
            src_ref=win.at[own], dst_ref=win.at[rows_of(2 * core, GROUP)],
            send_sem=hsend.at[a, 0], recv_sem=hrecv.at[a, 0],
            device_id=sibling, device_id_type=MESH,
        )
        far = pltpu.make_async_remote_copy(
            src_ref=win.at[own], dst_ref=win.at[rows_of(2 * (1 - core), GROUP)],
            send_sem=hsend.at[a, 1], recv_sem=hrecv.at[a, 1],
            device_id=beside, device_id_type=MESH,
        )
        return far, sib

    lane = lax.broadcasted_iota(jnp.int32, (1, 128), 1)

    def block(win, b):
        return win[rows_of(b, B), :]

    def pair(win, i, m):
        return jnp.concatenate([block(win, i + m - 1), block(win, i + m + TILES)], axis=1)

    def split(value, right, axis):
        low = value.astype(BF)
        left = jnp.where(right, 0.0, value).astype(BF)
        return jnp.concatenate([left, low - left], axis=axis)

    def pick(both, right):
        return jnp.where(right, both[:, HEAD_DIM:], both[:, :HEAD_DIM])

    def score_tile(i, c):
        q = q_own[rows_of(i, B), :]
        q32 = q.astype(F32)
        end = end_row[i]
        first = start_row[i]
        folded = first + FOLD * B
        peak = jnp.full((B, 128), NEG, F32)
        for m in range(FOLD):
            if m == 0:
                s = dot_nt(q, block(k_win, i + TILES))
            else:
                right = end > m * B
                s = dot_nt(split(q32, right, 1), pair(k_win, i, m))
                edge = jnp.where(right, end, folded)
                left = jnp.logical_not(right)
            for h in range(2):
                col = lane + (m * B + h * 128)
                if m == 0:
                    valid = (col < end) & (col >= first)
                else:
                    valid = jnp.logical_xor(col < edge, left)
                part = jnp.where(valid, s[:, h * 128:(h + 1) * 128], NEG)
                peak = jnp.maximum(peak, part)
                scores[i, m, :, h * 128:(h + 1) * 128] = part
        peaks[i] = jnp.broadcast_to(jnp.max(peak, axis=1, keepdims=True), (B, 128))
        return c

    def output_tile(i, c):
        end = end_row[i]
        peak = peaks[i]
        acc = jnp.zeros((B, HEAD_DIM), F32)
        mass = jnp.zeros((B, 128), F32)
        for m in range(FOLD):
            parts = []
            for h in range(2):
                p = jnp.exp2((scores[i, m, :, h * 128:(h + 1) * 128] - peak) * (SCALE * LOG2E))
                mass += p
                parts.append(p.astype(BF))
            low = jnp.concatenate(parts, axis=1)
            probs[i, m] = low
            if m == 0:
                acc += dot_nn(low, block(v_win, i + TILES))
            else:
                acc += pick(dot_nn(low, pair(v_win, i, m)), end > m * B)
        inv = 1.0 / jnp.sum(mass, axis=1, keepdims=True)
        invs[i] = jnp.broadcast_to(inv, (B, 128))
        att[rows_of(i, B), :] = (acc * inv).astype(BF)
        return c

    def add_pair(a, i, m, both):
        grads[a, i + m - 1] += both[:HEAD_DIM]
        grads[a, i + m + TILES] += both[HEAD_DIM:]

    def value_tile(i, c):
        scaled = (g_own[rows_of(i, B), :].astype(F32) * invs[i]).T
        end = end_lane[i][:1]
        grads[1, i + TILES] += dot_nn(scaled.astype(BF), probs[i, 0])
        for m in range(1, FOLD):
            add_pair(1, i, m, dot_nn(split(scaled, end > m * B, 0), probs[i, m]))
        return c

    def grad_tile(i):
        rows = rows_of(i, B)
        inv = invs[i]
        g32 = g_own[rows, :].astype(F32)
        dot = jnp.sum(g32 * att[rows, :].astype(F32), axis=1, keepdims=True)
        dot = jnp.broadcast_to(dot, (B, 128))
        scaled = (q_own[rows, :].astype(F32) * (inv * SCALE)).T
        end = end_row[i]
        ends = end_lane[i][:1]
        acc = jnp.zeros((B, HEAD_DIM), F32)
        for m in range(FOLD):
            if m == 0:
                dp = dot_nt(g_own[rows, :], block(v_win, i + TILES))
            else:
                right = end > m * B
                dp = dot_nt(split(g32, right, 1), pair(v_win, i, m))
            ds = jnp.concatenate(
                [
                    (
                        probs[i, m, :, h * 128:(h + 1) * 128].astype(F32)
                        * (dp[:, h * 128:(h + 1) * 128] - dot)
                    ).astype(BF)
                    for h in range(2)
                ],
                axis=1,
            )
            if m == 0:
                acc += dot_nn(ds, block(k_win, i + TILES))
                grads[0, i + TILES] += dot_nn(scaled.astype(BF), ds)
            else:
                acc += pick(dot_nn(ds, pair(k_win, i, m)), right)
                add_pair(0, i, m, dot_nn(split(scaled, ends > m * B, 0), ds))
        dq[rows, :] = (acc * (inv * SCALE)).astype(BF)

    outs = (att_out, dq_out, dk_out, dv_out)
    ready = (att, dq, total.at[0], total.at[1])

    def out_refs(a, s):
        return ready[a].at[rows_of(s, PIECE)], outs[a].at[:, rows_of(my_head, HEAD_DIM)]

    def out_copy(a, s, owner):
        src, dst = out_refs(a, s)
        return pltpu.make_async_remote_copy(
            src_ref=src, dst_ref=dst, send_sem=osend.at[a, s], recv_sem=orecv.at[a, my_head],
            device_id=owner, device_id_type=MESH,
        )

    def start_out(a, s):
        mine, owner = owner_of(s)

        @pl.when(mine)
        def _():
            src, dst = out_refs(a, s)
            pltpu.make_async_copy(src, dst, orecv.at[a, my_head]).start()

        @pl.when(jnp.logical_not(mine))
        def _():
            out_copy(a, s, owner).start()

    def far_copy(a, t):
        return pltpu.make_async_remote_copy(
            src_ref=far_buf.at[a, t], dst_ref=far_in.at[a, t],
            send_sem=fsend.at[a, t], recv_sem=frecv.at[a, t],
            device_id=beside, device_id_type=MESH,
        )

    def send_far(a, t):
        far_buf[a, t] = grads[a, t + 2 * TILES * core].astype(BF)
        far_copy(a, t).start()

    def sib_copy(a):
        return pltpu.make_async_remote_copy(
            src_ref=sib_buf.at[a], dst_ref=sib_in.at[a],
            send_sem=ssend.at[a], recv_sem=srecv.at[a],
            device_id=sibling, device_id_type=MESH,
        )

    def send_sib(a):
        def fill(t, c):
            sib_buf[a, t] = grads[a, t + 2 * TILES * (1 - core)].astype(BF)
            return c

        lax.fori_loop(0, TILES, fill, 0)
        sib_copy(a).start()

    def finish(a):
        sib_copy(a).wait_recv()

        def add(t, c):
            far_copy(a, t).wait_recv()
            value = grads[a, t + TILES] + far_in[a, t].astype(F32) + sib_in[a, t].astype(F32)
            total[a, rows_of(t, B), :] = value.T.astype(BF)
            start_out(2 + a, 2 * t)
            start_out(2 + a, 2 * t + 1)
            return c

        lax.fori_loop(0, TILES, add, 0)

    wait_in(0)
    k_halo = halo_copies(0, k_win)
    for copy in k_halo:
        copy.start()
    wait_in(1)
    for copy in k_halo:
        copy.wait_recv()
    lax.fori_loop(0, TILES, score_tile, 0)
    wait_in(2)
    v_halo = halo_copies(1, v_win)
    for copy in v_halo:
        copy.start()
    for copy in v_halo:
        copy.wait_recv()
    lax.fori_loop(0, TILES, output_tile, 0)
    wait_in(3)

    def start_att(s, c):
        start_out(0, s)
        return c

    lax.fori_loop(0, PIECES, start_att, 0)
    lax.fori_loop(0, TILES, value_tile, 0)

    def far_values(t, c):
        send_far(1, t)
        return c

    lax.fori_loop(0, TILES, far_values, 0)
    send_sib(1)

    def grad_step(n, c):
        i = jnp.where(core == 0, n, TILES - 1 - n)
        grad_tile(i)
        start_out(1, 2 * i)
        start_out(1, 2 * i + 1)
        send_far(0, i)

        @pl.when(n == 3)
        def _():
            finish(1)

        return c

    lax.fori_loop(0, TILES, grad_step, 0)
    send_sib(0)
    finish(0)

    for copy in k_halo + v_halo:
        copy.wait_send()
    for a in range(2):
        sib_copy(a).wait_send()

        def wait_far(t, c):
            far_copy(a, t).wait_send()
            return c

        lax.fori_loop(0, TILES, wait_far, 0)
    for a in range(4):

        @pl.when(half != core)
        def _():
            in_copy(a, 0).wait_send()

        def wait_in_sent(step, c):
            in_copy(a, step).wait_send()
            return c

        lax.fori_loop(1, PIECES, wait_in_sent, 0)

        def wait_out(h, c):
            part = outs[a].at[:, rows_of(h, HEAD_DIM)]
            pltpu.make_async_copy(part, part, orecv.at[a, h]).wait()
            mine, owner = owner_of(h)

            @pl.when(jnp.logical_not(mine))
            def _():
                out_copy(a, h, owner).wait_send()

            return c

        lax.fori_loop(0, PIECES, wait_out, 0)


def body(queries, keys_in, values, out_grad, doc_lengths):
    any_spec = pl.BlockSpec(memory_space=pl.ANY)
    out = jax.ShapeDtypeStruct((PIECE, PIECES * HEAD_DIM), BF)
    own = pltpu.VMEM((GROUP, HEAD_DIM), BF)
    window = pltpu.VMEM((3 * GROUP, HEAD_DIM), BF)
    side = pltpu.VMEM((2, TILES, HEAD_DIM, B), BF)
    dma = pltpu.SemaphoreType.DMA
    return pl.pallas_call(
        kernel,
        out_shape=(out,) * 4,
        in_specs=[pl.BlockSpec(memory_space=pltpu.SMEM)] + [any_spec] * 4,
        out_specs=(any_spec,) * 4,
        scratch_shapes=[
            own, own, window, window,
            pltpu.VMEM((TILES, FOLD, B, B), F32),
            pltpu.VMEM((TILES, FOLD, B, B), BF),
            pltpu.VMEM((TILES, B, 128), jnp.int32),
            pltpu.VMEM((TILES, B, 128), jnp.int32),
            pltpu.VMEM((TILES, 8, B), jnp.int32),
            pltpu.VMEM((TILES, B, 128), F32),
            pltpu.VMEM((TILES, B, 128), F32),
            own, own,
            pltpu.VMEM((2, 3 * TILES, HEAD_DIM, B), F32),
            side, side, side, side,
            pltpu.VMEM((2, GROUP, HEAD_DIM), BF),
            dma((4, PIECES)), dma((4, PIECES)), dma((2, 2)), dma((2, 2)),
            dma((4, PIECES)), dma((4, PIECES)), dma((2, TILES)), dma((2, TILES)),
            dma((2,)), dma((2,)),
        ],
        compiler_params=pltpu.CompilerParams(
            collective_id=0, has_side_effects=True, vmem_limit_bytes=60 * 1024 * 1024
        ),
        name="attend",
    )(doc_lengths, queries, keys_in, values, out_grad)


def solution(mesh):
    tokens = P(("ctx", "head"), None)
    return jax.shard_map(
        body,
        mesh=mesh,
        in_specs=(tokens,) * 4 + (P(),),
        out_specs=(tokens,) * 4,
        check_vma=False,
    )
```

profile of v0, /device:TPU:1, one launch (start us, length us, event | category | flops | bytes accessed | tf_op | source)
XLA Modules:
  0.0 91.6 jit_solution(9739020692345683870)
XLA Ops:
  0.6 85.8 %attend.1 = (bf16[128,2048]{1,0:T(8,128)(2,1)}, bf16[128,2048]{1,0:T(8,128)(2,1)}, bf16[128,2048]{1,0:T(8,128)(2,1)}, bf16[128,2048]{1,0:T(8,128)(2,1)}) custom-call(s32[15]{0:T(128)} %lens.1, bf16[128,2048]{1,0:T(8,128)(2,1)} %q_in.1, bf16[128,2048]{1,0:T(8,128)(2,1)} %k_in.1, bf16[128,2048]{1,0:T(8,128)(2,1)} %v_in.1, bf16[128,2048]{1,0:T(8,128)(2,1)} %g_in.1), custom_call_target="tpu_custom_call" | custom-call | tf_op jit(solution)/shard_map/attend/pallas_call | solution.py:437
  86.4 0.0 copy-start.2
  86.4 1.9 %copy.13 = bf16[128,2048]{1,0:T(8,128)(2,1)} copy(bf16[128,2048]{1,0:T(8,128)(2,1)} %get-tuple-element.8) | data formatting | bytes 1048576
  88.3 0.0 copy-done.2
  88.4 0.0 copy-start.1
  88.4 0.8 copy.14
  89.1 0.4 copy-done.1
  89.6 0.0 copy-start
  89.6 0.8 copy.15
  90.4 0.4 copy-done
  90.8 0.8 copy.16
Async XLA Ops:
  86.4 2.0 %copy-start.2 = (bf16[128,2048]{1,0:T(8,128)(2,1)S(1)}, bf16[128,2048]{1,0:T(8,128)(2,1)}, u32[]{:S(2)}) copy-start(bf16[128,2048]{1,0:T(8,128)(2,1)} %get-tuple-element.9) | copy-start | bytes 1572868
  88.4 1.2 %copy-start.1 = (bf16[128,2048]{1,0:T(8,128)(2,1)S(1)}, bf16[128,2048]{1,0:T(8,128)(2,1)}, u32[]{:S(2)}) copy-start(bf16[128,2048]{1,0:T(8,128)(2,1)} %get-tuple-element.10) | copy-start | bytes 1572868
  89.6 1.2 %copy-start = (bf16[128,2048]{1,0:T(8,128)(2,1)S(1)}, bf16[128,2048]{1,0:T(8,128)(2,1)}, u32[]{:S(2)}) copy-start(bf16[128,2048]{1,0:T(8,128)(2,1)} %get-tuple-element.11) | copy-start | bytes 1572868
where the time goes:
time: 91.9 us; the launch traced here: 91.6 us
  Pallas kernels  85.8 us (93%)
  local copies, waits for them, and re-layouts  5.19 us (6%)
    pallas_call x1, Pallas kernels, body(): pl.pallas_call(kernel, out_shape=(out,) * 4, in_specs=[pl.BlockSpec(memor...  85.8 us
    unnamed x10, local copies, waits for them, and re-layouts  5.19 us

commit v1 on v0

--- a/solution.py
+++ b/solution.py
@@ -10,6 +10,8 @@
 GROUP = 2048
 PIECE = 128
 PIECES = GROUP // PIECE
+CHUNKS = 4
+CHUNK = GROUP // CHUNKS
 B = 256
 TILES = GROUP // B
 FOLD = TILES + 1
@@ -63,12 +65,6 @@
         return mine, {"ctx": ctx_of(x, zz, cc), "head": yy}
 
     def greet(step, c):
-        _, host = host_of(step)
-
-        @pl.when((step > 0) | (half != core))
-        def _():
-            pl.semaphore_signal(barrier, inc=1, device_id=host, device_id_type=MESH)
-
         mine, owner = owner_of(step)
 
         @pl.when(jnp.logical_not(mine))
@@ -80,7 +76,7 @@
     lax.fori_loop(0, PIECES, greet, 0)
     pl.semaphore_signal(barrier, inc=1, device_id=sibling, device_id_type=MESH)
     pl.semaphore_signal(barrier, inc=1, device_id=beside, device_id_type=MESH)
-    pl.semaphore_wait(barrier, 2 * jnp.where(half == core, PIECES - 1, PIECES) + 2)
+    pl.semaphore_wait(barrier, jnp.where(half == core, PIECES - 1, PIECES) + 2)
 
     def rows_of(s, count):
         return pl.ds(pl.multiple_of(s * count, count), count)
@@ -100,8 +96,7 @@
             device_id=host, device_id_type=MESH,
         )
 
-    for a in range(4):
-
+    def start_in_all(a):
         @pl.when(half == core)
         def _():
             src, dst, _ = in_refs(a, 0)
@@ -116,6 +111,9 @@
             return c
 
         lax.fori_loop(1, PIECES, start_in, 0)
+
+    for a in (0, 2, 1, 3):
+        start_in_all(a)
 
     bound = -((ctx // 8) * 2 + core) * GROUP
     bounds = [bound]
@@ -147,26 +145,51 @@
 
     lax.fori_loop(0, 3 * TILES, clear, 0)
 
+    def wait_piece(a, s):
+        piece = incoming[a].at[rows_of(s, PIECE)]
+        pltpu.make_async_copy(piece, piece, recv.at[a, s]).wait()
+
     def wait_in(a):
         def wait(s, c):
-            piece = incoming[a].at[rows_of(s, PIECE)]
-            pltpu.make_async_copy(piece, piece, recv.at[a, s]).wait()
+            wait_piece(a, s)
             return c
 
         lax.fori_loop(0, PIECES, wait, 0)
 
-    def halo_copies(a, win):
+    order = jnp.where((z - 2 * core) % 4 == 0, 0, 2)
+
+    def halo_copies(a, n):
+        win = (k_win, v_win)[a]
+        chunk = (order + n) % CHUNKS
+        src = win.at[rows_of(CHUNKS + chunk, CHUNK)]
         sib = pltpu.make_async_remote_copy(
-            src_ref=win.at[own], dst_ref=win.at[rows_of(2 * core, GROUP)],
-            send_sem=hsend.at[a, 0], recv_sem=hrecv.at[a, 0],
+            src_ref=src, dst_ref=win.at[rows_of(2 * core * CHUNKS + chunk, CHUNK)],
+            send_sem=hsend.at[a, 0, chunk], recv_sem=hrecv.at[a, 0, chunk],
             device_id=sibling, device_id_type=MESH,
         )
         far = pltpu.make_async_remote_copy(
-            src_ref=win.at[own], dst_ref=win.at[rows_of(2 * (1 - core), GROUP)],
-            send_sem=hsend.at[a, 1], recv_sem=hrecv.at[a, 1],
+            src_ref=src, dst_ref=win.at[rows_of(2 * (1 - core) * CHUNKS + chunk, CHUNK)],
+            send_sem=hsend.at[a, 1, chunk], recv_sem=hrecv.at[a, 1, chunk],
             device_id=beside, device_id_type=MESH,
         )
         return far, sib
+
+    def pass_on(a, n):
+        def wait(s, c):
+            wait_piece(2 * a, (order + n) % CHUNKS * CHUNKS + s)
+            return c
+
+        lax.fori_loop(0, CHUNKS, wait, 0)
+        for copy in halo_copies(a, n):
+            copy.start()
+
+    def wait_halo(a):
+        def wait(n, c):
+            for copy in halo_copies(a, n):
+                copy.wait_recv()
+            return c
+
+        lax.fori_loop(0, CHUNKS, wait, 0)
 
     lane = lax.broadcasted_iota(jnp.int32, (1, 128), 1)
 
@@ -184,7 +207,7 @@
     def pick(both, right):
         return jnp.where(right, both[:, HEAD_DIM:], both[:, :HEAD_DIM])
 
-    def score_tile(i, c):
+    def score_tile(i):
         q = q_own[rows_of(i, B), :]
         q32 = q.astype(F32)
         end = end_row[i]
@@ -197,21 +220,20 @@
             else:
                 right = end > m * B
                 s = dot_nt(split(q32, right, 1), pair(k_win, i, m))
-                edge = jnp.where(right, end, folded)
-                left = jnp.logical_not(right)
+                sign = jnp.where(right, 1.0, -1.0)
+                edge = jnp.where(right, -end, folded - 1).astype(F32)
             for h in range(2):
                 col = lane + (m * B + h * 128)
                 if m == 0:
                     valid = (col < end) & (col >= first)
                 else:
-                    valid = jnp.logical_xor(col < edge, left)
+                    valid = (col.astype(F32) * sign + edge) < 0.0
                 part = jnp.where(valid, s[:, h * 128:(h + 1) * 128], NEG)
                 peak = jnp.maximum(peak, part)
                 scores[i, m, :, h * 128:(h + 1) * 128] = part
         peaks[i] = jnp.broadcast_to(jnp.max(peak, axis=1, keepdims=True), (B, 128))
-        return c
-
-    def output_tile(i, c):
+
+    def output_tile(i):
         end = end_row[i]
         peak = peaks[i]
         acc = jnp.zeros((B, HEAD_DIM), F32)
@@ -231,19 +253,17 @@
         inv = 1.0 / jnp.sum(mass, axis=1, keepdims=True)
         invs[i] = jnp.broadcast_to(inv, (B, 128))
         att[rows_of(i, B), :] = (acc * inv).astype(BF)
-        return c
 
     def add_pair(a, i, m, both):
         grads[a, i + m - 1] += both[:HEAD_DIM]
         grads[a, i + m + TILES] += both[HEAD_DIM:]
 
-    def value_tile(i, c):
+    def value_tile(i):
         scaled = (g_own[rows_of(i, B), :].astype(F32) * invs[i]).T
         end = end_lane[i][:1]
         grads[1, i + TILES] += dot_nn(scaled.astype(BF), probs[i, 0])
         for m in range(1, FOLD):
             add_pair(1, i, m, dot_nn(split(scaled, end > m * B, 0), probs[i, m]))
-        return c
 
     def grad_tile(i):
         rows = rows_of(i, B)
@@ -259,24 +279,18 @@
             if m == 0:
                 dp = dot_nt(g_own[rows, :], block(v_win, i + TILES))
             else:
-                right = end > m * B
-                dp = dot_nt(split(g32, right, 1), pair(v_win, i, m))
-            ds = jnp.concatenate(
-                [
-                    (
-                        probs[i, m, :, h * 128:(h + 1) * 128].astype(F32)
-                        * (dp[:, h * 128:(h + 1) * 128] - dot)
-                    ).astype(BF)
-                    for h in range(2)
-                ],
-                axis=1,
-            )
-            if m == 0:
-                acc += dot_nn(ds, block(k_win, i + TILES))
-                grads[0, i + TILES] += dot_nn(scaled.astype(BF), ds)
-            else:
-                acc += pick(dot_nn(ds, pair(k_win, i, m)), right)
-                add_pair(0, i, m, dot_nn(split(scaled, ends > m * B, 0), ds))
+                dp = dot_nt(split(g32, end > m * B, 1), pair(v_win, i, m))
+            for h in range(2):
+                half_cols = slice(h * 128, (h + 1) * 128)
+                probs[i, m, :, half_cols] = (
+                    probs[i, m, :, half_cols].astype(F32) * (dp[:, half_cols] - dot)
+                ).astype(BF)
+        acc = dot_nn(probs[i, 0], block(k_win, i + TILES))
+        for m in range(1, FOLD):
+            acc += pick(dot_nn(probs[i, m], pair(k_win, i, m)), end > m * B)
+        grads[0, i + TILES] += dot_nn(scaled.astype(BF), probs[i, 0])
+        for m in range(1, FOLD):
+            add_pair(0, i, m, dot_nn(split(scaled, ends > m * B, 0), probs[i, m]))
         dq[rows, :] = (acc * (inv * SCALE)).astype(BF)
 
     outs = (att_out, dq_out, dk_out, dv_out)
@@ -315,26 +329,25 @@
         far_buf[a, t] = grads[a, t + 2 * TILES * core].astype(BF)
         far_copy(a, t).start()
 
-    def sib_copy(a):
+    def sib_copy(a, t):
         return pltpu.make_async_remote_copy(
-            src_ref=sib_buf.at[a], dst_ref=sib_in.at[a],
-            send_sem=ssend.at[a], recv_sem=srecv.at[a],
+            src_ref=sib_buf.at[a, t], dst_ref=sib_in.at[a, t],
+            send_sem=ssend.at[a, t], recv_sem=srecv.at[a, t],
             device_id=sibling, device_id_type=MESH,
         )
 
     def send_sib(a):
         def fill(t, c):
             sib_buf[a, t] = grads[a, t + 2 * TILES * (1 - core)].astype(BF)
+            sib_copy(a, t).start()
             return c
 
         lax.fori_loop(0, TILES, fill, 0)
-        sib_copy(a).start()
 
     def finish(a):
-        sib_copy(a).wait_recv()
-
         def add(t, c):
             far_copy(a, t).wait_recv()
+            sib_copy(a, t).wait_recv()
             value = grads[a, t + TILES] + far_in[a, t].astype(F32) + sib_in[a, t].astype(F32)
             total[a, rows_of(t, B), :] = value.T.astype(BF)
             start_out(2 + a, 2 * t)
@@ -343,45 +356,57 @@
 
         lax.fori_loop(0, TILES, add, 0)
 
-    wait_in(0)
-    k_halo = halo_copies(0, k_win)
-    for copy in k_halo:
-        copy.start()
+    def ordered(n):
+        return jnp.where(core == 0, n, TILES - 1 - n)
+
+    def key_step(n, c):
+        pass_on(0, n)
+        return c
+
+    lax.fori_loop(0, CHUNKS, key_step, 0)
+
+    def val_step(n, c):
+        pass_on(1, n)
+        return c
+
+    lax.fori_loop(0, CHUNKS, val_step, 0)
     wait_in(1)
-    for copy in k_halo:
-        copy.wait_recv()
-    lax.fori_loop(0, TILES, score_tile, 0)
-    wait_in(2)
-    v_halo = halo_copies(1, v_win)
-    for copy in v_halo:
-        copy.start()
-    for copy in v_halo:
-        copy.wait_recv()
-    lax.fori_loop(0, TILES, output_tile, 0)
+    wait_halo(0)
+
+    def score_step(i, c):
+        score_tile(i)
+
+        return c
+
+    lax.fori_loop(0, TILES, score_step, 0)
+    wait_halo(1)
+
+    def output_step(i, c):
+        output_tile(i)
+        start_out(0, 2 * i)
+        start_out(0, 2 * i + 1)
+        return c
+
+    lax.fori_loop(0, TILES, output_step, 0)
     wait_in(3)
 
-    def start_att(s, c):
-        start_out(0, s)
-        return c
-
-    lax.fori_loop(0, PIECES, start_att, 0)
-    lax.fori_loop(0, TILES, value_tile, 0)
-
-    def far_values(t, c):
-        send_far(1, t)
-        return c
-
-    lax.fori_loop(0, TILES, far_values, 0)
+    def value_step(n, c):
+        i = ordered(n)
+        value_tile(i)
+        send_far(1, i)
+        return c
+
+    lax.fori_loop(0, TILES, value_step, 0)
     send_sib(1)
 
     def grad_step(n, c):
-        i = jnp.where(core == 0, n, TILES - 1 - n)
+        i = ordered(n)
         grad_tile(i)
         start_out(1, 2 * i)
         start_out(1, 2 * i + 1)
         send_far(0, i)
 
-        @pl.when(n == 3)
+        @pl.when(n == 2)
         def _():
             finish(1)
 
@@ -391,16 +416,21 @@
     send_sib(0)
     finish(0)
 
-    for copy in k_halo + v_halo:
-        copy.wait_send()
     for a in range(2):
-        sib_copy(a).wait_send()
-
-        def wait_far(t, c):
+
+        def wait_halo_sent(n, c):
+            for copy in halo_copies(a, n):
+                copy.wait_send()
+            return c
+
+        lax.fori_loop(0, CHUNKS, wait_halo_sent, 0)
+
+        def wait_sides(t, c):
             far_copy(a, t).wait_send()
-            return c
-
-        lax.fori_loop(0, TILES, wait_far, 0)
+            sib_copy(a, t).wait_send()
+            return c
+
+        lax.fori_loop(0, TILES, wait_sides, 0)
     for a in range(4):
 
         @pl.when(half != core)
@@ -425,6 +455,11 @@
             return c
 
         lax.fori_loop(0, PIECES, wait_out, 0)
+
+
+def place(*refs):
+    for a in range(4):
+        refs[4 + a][...] = refs[a][...]
 
 
 def body(queries, keys_in, values, out_grad, doc_lengths):
@@ -434,7 +469,7 @@
     window = pltpu.VMEM((3 * GROUP, HEAD_DIM), BF)
     side = pltpu.VMEM((2, TILES, HEAD_DIM, B), BF)
     dma = pltpu.SemaphoreType.DMA
-    return pl.pallas_call(
+    results = pl.pallas_call(
         kernel,
         out_shape=(out,) * 4,
         in_specs=[pl.BlockSpec(memory_space=pltpu.SMEM)] + [any_spec] * 4,
@@ -452,15 +487,19 @@
             pltpu.VMEM((2, 3 * TILES, HEAD_DIM, B), F32),
             side, side, side, side,
             pltpu.VMEM((2, GROUP, HEAD_DIM), BF),
-            dma((4, PIECES)), dma((4, PIECES)), dma((2, 2)), dma((2, 2)),
+            dma((4, PIECES)), dma((4, PIECES)), dma((2, 2, CHUNKS)), dma((2, 2, CHUNKS)),
             dma((4, PIECES)), dma((4, PIECES)), dma((2, TILES)), dma((2, TILES)),
-            dma((2,)), dma((2,)),
+            dma((2, TILES)), dma((2, TILES)),
         ],
         compiler_params=pltpu.CompilerParams(
             collective_id=0, has_side_effects=True, vmem_limit_bytes=60 * 1024 * 1024
         ),
         name="attend",
     )(doc_lengths, queries, keys_in, values, out_grad)
+    rows = pl.BlockSpec((PIECE // 2, PIECES * HEAD_DIM), lambda i: (i, 0))
+    return pl.pallas_call(
+        place, grid=(2,), out_shape=(out,) * 4, in_specs=[rows] * 4, out_specs=(rows,) * 4, name="place"
+    )(*results)
 
 
 def solution(mesh):

time: 91.9 us -> 78 us (0.85)
  Pallas kernels: 85.8 us -> 76.7 us
  local copies, waits for them, and re-layouts: 5.19 us -> 0 us
    pallas_call x1, Pallas kernels: 85.8 us -> 74.1 us  [body(): pl.pallas_call(kernel, out_shape=(out,) * 4, in_specs=[pl.BlockSpec(memor...]
    unnamed x10 -> x0, local copies, waits for them, and re-layouts: 5.19 us -> none
    pallas_call x0 -> x1, Pallas kernels: none -> 2.58 us  [body(): pl.pallas_call(place, grid=(2,), out_shape=(out,) * 4, in_specs=[rows] *...]
where the time goes in v1:
time: 78 us; the launch traced here: 77.3 us
  Pallas kernels  76.7 us (98%)
    pallas_call x1, Pallas kernels, body(): pl.pallas_call(kernel, out_shape=(out,) * 4, in_specs=[pl.BlockSpec(memor...  74.1 us
    pallas_call x1, Pallas kernels, body(): pl.pallas_call(place, grid=(2,), out_shape=(out,) * 4, in_specs=[rows] *...  2.58 us

profile of v1, /device:TPU:1, one launch (start us, length us, event | category | flops | bytes accessed | tf_op | source)
XLA Modules:
  0.0 77.3 jit_solution(9280122836193911163)
XLA Ops:
  0.6 74.1 %attend.1 = (bf16[128,2048]{1,0:T(8,128)(2,1)}, bf16[128,2048]{1,0:T(8,128)(2,1)}, bf16[128,2048]{1,0:T(8,128)(2,1)}, bf16[128,2048]{1,0:T(8,128)(2,1)}) custom-call(s32[15]{0:T(128)} %lens.1, bf16[128,2048]{1,0:T(8,128)(2,1)} %q_in.1, bf16[128,2048]{1,0:T(8,128)(2,1)} %k_in.1, bf16[128,2048]{1,0:T(8,128)(2,1)} %v_in.1, bf16[128,2048]{1,0:T(8,128)(2,1)} %g_in.1), custom_call_target="tpu_custom_call" | custom-call | tf_op jit(solution)/shard_map/attend/pallas_call | solution.py:472
  74.7 2.6 %place.1 = (bf16[128,2048]{1,0:T(8,128)(2,1)}, bf16[128,2048]{1,0:T(8,128)(2,1)}, bf16[128,2048]{1,0:T(8,128)(2,1)}, bf16[128,2048]{1,0:T(8,128)(2,1)}) custom-call(bf16[128,2048]{1,0:T(8,128)(2,1)} %get-tuple-element.8.refs_0_, bf16[128,2048]{1,0:T(8,128)(2,1)} %get-tuple-element.9.refs_1_, bf16[128,2048]{1,0:T(8,128)(2,1)} %get-tuple-element.10.refs_2_, ...), custom_call_target="tpu_custom_call" | custom-call | tf_op jit(solution)/shard_map/place/pallas_call | solution.py:500

commit v2 on v1

--- a/solution.py
+++ b/solution.py
@@ -282,9 +282,7 @@
                 dp = dot_nt(split(g32, end > m * B, 1), pair(v_win, i, m))
             for h in range(2):
                 half_cols = slice(h * 128, (h + 1) * 128)
-                probs[i, m, :, half_cols] = (
-                    probs[i, m, :, half_cols].astype(F32) * (dp[:, half_cols] - dot)
-                ).astype(BF)
+                probs[i, m, :, half_cols] *= (dp[:, half_cols] - dot).astype(BF)
         acc = dot_nn(probs[i, 0], block(k_win, i + TILES))
         for m in range(1, FOLD):
             acc += pick(dot_nn(probs[i, m], pair(k_win, i, m)), end > m * B)
@@ -378,7 +376,7 @@
 
         return c
 
-    lax.fori_loop(0, TILES, score_step, 0)
+    lax.fori_loop(0, TILES, score_step, 0, unroll=2)
     wait_halo(1)
 
     def output_step(i, c):

time: 78 us -> 77.4 us (level)
  no operation moved by 1% of the time
where the time goes in v2:
time: 77.4 us; the launch traced here: 76.6 us
  Pallas kernels  76 us (98%)
    pallas_call x1, Pallas kernels, body(): pl.pallas_call(kernel, out_shape=(out,) * 4, in_specs=[pl.BlockSpec(memor...  73.4 us
    pallas_call x1, Pallas kernels, body(): pl.pallas_call(place, grid=(2,), out_shape=(out,) * 4, in_specs=[rows] *...  2.58 us

profile of v2, /device:TPU:1, one launch (start us, length us, event | category | flops | bytes accessed | tf_op | source)
XLA Modules:
  0.0 76.6 jit_solution(11950345048599864436)
XLA Ops:
  0.6 73.4 %attend.1 = (bf16[128,2048]{1,0:T(8,128)(2,1)}, bf16[128,2048]{1,0:T(8,128)(2,1)}, bf16[128,2048]{1,0:T(8,128)(2,1)}, bf16[128,2048]{1,0:T(8,128)(2,1)}) custom-call(s32[15]{0:T(128)} %lens.1, bf16[128,2048]{1,0:T(8,128)(2,1)} %q_in.1, bf16[128,2048]{1,0:T(8,128)(2,1)} %k_in.1, bf16[128,2048]{1,0:T(8,128)(2,1)} %v_in.1, bf16[128,2048]{1,0:T(8,128)(2,1)} %g_in.1), custom_call_target="tpu_custom_call" | custom-call | tf_op jit(solution)/shard_map/attend/pallas_call | solution.py:470
  74.1 2.6 %place.1 = (bf16[128,2048]{1,0:T(8,128)(2,1)}, bf16[128,2048]{1,0:T(8,128)(2,1)}, bf16[128,2048]{1,0:T(8,128)(2,1)}, bf16[128,2048]{1,0:T(8,128)(2,1)}) custom-call(bf16[128,2048]{1,0:T(8,128)(2,1)} %get-tuple-element.8.refs_0_, bf16[128,2048]{1,0:T(8,128)(2,1)} %get-tuple-element.9.refs_1_, bf16[128,2048]{1,0:T(8,128)(2,1)} %get-tuple-element.10.refs_2_, ...), custom_call_target="tpu_custom_call" | custom-call | tf_op jit(solution)/shard_map/place/pallas_call | solution.py:498
